TPU v7x, 512 devices: a whole 4x8x8 slice. The times are simulated.
512 devices in a mesh: row: 32 (over x, z), col: 16 (over y, core).
Axes of the slice: x: 4, y: 8, z: 8, core: 2. Of those that a mesh axis runs over, the one named last changes fastest.
Arguments:
- prior_solved: float32 [49152, 512], P('row', 'col'), may hold values from -6 to 6
- block_one: float32 [2048, 49152], P('col', 'row'), may hold values from -0.02734375 to 0.02734375
- block_two: float32 [2048, 49152], P('col', 'row'), may hold values from -0.02734375 to 0.02734375
- cross_block: float32 [2048, 2048], P('col', 'row'), may hold values from -0.125 to 0.125
- inverse_one: float32 [2048, 2048], P('row', 'col'), may hold values from -1 to 2, as said below
- inverse_two: float32 [2048, 2048], P('row', 'col'), may hold values from -1 to 2, as said below
- rhs_one: float32 [2048, 512], P('col', 'row'), may hold values from -6 to 6
- rhs_two: float32 [2048, 512], P('col', 'row'), may hold values from -6 to 6
Outputs:
- solved_one: float32 [2048, 512], P('col', 'row')
- solved_two: float32 [2048, 512], P('col', 'row')
Inputs may be any that keep to these rules, and one draw needn't show every extreme that they name: `inverse_one`: lower triangular: zero above the diagonal. `inverse_two`: lower triangular: zero above the diagonal.
All inputs are finite; a program needn't handle non-finite values.
Results may differ from a plain program's by a relative error of at most 0.00011.
Values sent between devices are 32-bit elements; how exact they have to be, the bound alone decides.
A program may use at most 64 MiB of HBM per device.

v0:
```python
import jax
import jax.numpy as jnp
from jax import lax
from jax.sharding import PartitionSpec as P


def diagonal_terms(inverse_cols, residual):
    return jnp.dot(
        inverse_cols, residual, precision=lax.Precision.HIGHEST, preferred_element_type=jnp.float32
    )


def per_device(
    prior_solved, block_one, block_two, cross_block, inverse_one, inverse_two, rhs_one, rhs_two
):
    highest = lax.Precision.HIGHEST
    inv_one_cols, inv_two_cols, cross_rows = (
        lax.all_gather(inverse_one, "row", axis=0, tiled=True),
        lax.all_gather(inverse_two, "row", axis=0, tiled=True),
        lax.all_gather(cross_block, "row", axis=1, tiled=True),
    )
    column_piece = lax.all_gather(prior_solved, "col", axis=1, tiled=True)
    upper_term = jnp.dot(
        block_one, column_piece, precision=highest, preferred_element_type=jnp.float32
    )
    lower_term = jnp.dot(
        block_two, column_piece, precision=highest, preferred_element_type=jnp.float32
    )
    partials = jnp.stack([upper_term, lower_term])
    first_sum = lax.psum_scatter(partials[0], "row", scatter_dimension=1, tiled=True)
    residual_one = rhs_one - first_sum
    solved_one = lax.psum_scatter(
        diagonal_terms(inv_one_cols, residual_one), "col", scatter_dimension=0, tiled=True
    )
    solved_full = lax.all_gather(solved_one, "col", axis=0, tiled=True)
    second_sum = lax.psum_scatter(partials[1], "row", scatter_dimension=1, tiled=True)
    coupled = jnp.dot(
        cross_rows, solved_full, precision=highest, preferred_element_type=jnp.float32
    )
    residual_two = rhs_two - second_sum - coupled
    solved_two = lax.psum_scatter(
        diagonal_terms(inv_two_cols, residual_two), "col", scatter_dimension=0, tiled=True
    )
    return (solved_one, solved_two)


def solution(mesh):
    placed = (
        P("row", "col"),
        P("col", "row"),
        P("col", "row"),
        P("col", "row"),
        P("row", "col"),
        P("row", "col"),
        P("col", "row"),
        P("col", "row"),
    )
    return jax.shard_map(
        per_device,
        mesh=mesh,
        in_specs=placed,
        out_specs=(P("col", "row"), P("col", "row")),
        check_vma=False,
    )
```

profile of v0, /device:TPU:1, one launch (start us, length us, event | category | flops | bytes accessed | tf_op | source)
XLA Modules:
  0.0 878.7 jit_solution(12356310816868015099)
XLA Ops:
  7.2 0.7 all-gather.5.cloned.1.call-update
  8.0 0.7 all-gather.7.cloned.1.call-update
  8.7 0.0 reduce-scatter.5.cloned.1.call-start
  8.7 50.9 %all-gather.5.cloned.1.call-done = f32[1536,512]{0,1:T(8,128)} async-done(((f32[1536,32]{0,1:T(8,128)}), f32[1536,512]{0,1:T(8,128)}) %all-gather.5.cloned.1.call-update) | async-done | bytes 3145744 | tf_op jit(solution)/shard_map/all_gather | solution.py:22
  59.6 5.2 fusion.2
  64.8 0.0 reduce-scatter.7.cloned.1.call-start
  64.9 74.2 %all-gather.7.cloned.1.call-done = f32[2048,128]{1,0:T(8,128)} async-done(((f32[64,128]{1,0:T(8,128)}), f32[2048,128]{1,0:T(8,128)}) %all-gather.7.cloned.1.call-update) | async-done | bytes 1048592 | tf_op jit(solution)/shard_map/all_gather | solution.py:18
  139.1 221.1 %reduce-scatter.5.cloned.1.call-done = f32[128,16]{0,1:T(8,128)} async-done(((f32[128,512]{0,1:T(8,128)}), f32[128,16]{0,1:T(8,128)}) %reduce-scatter.5.cloned.1.call-update) | async-done | bytes 8208 | tf_op jit(solution)/shard_map/reduce_scatter | solution.py:30
  360.2 2.9 convolution_bitcast_fusion.1
  363.1 0.0 all-gather.9.cloned.1.call-start
  363.1 0.5 all-gather.9.cloned.1.call-update
  363.7 0.0 reduce-scatter.9.cloned.1.call-start
  363.7 5.2 fusion.3
  369.0 0.0 all-gather.11.cloned.1.call-start
  369.0 0.7 all-gather.11.cloned.1.call-update
  369.7 0.0 reduce-scatter.11.cloned.1.call-start
  369.8 53.3 %reduce-scatter.7.cloned.1.call-done = f32[128,16]{0,1:T(8,128)} async-done(((f32[2048,16]{0,1:T(8,128)}), f32[128,16]{0,1:T(8,128)}) %reduce-scatter.7.cloned.1.call-update) | async-done | bytes 8208 | tf_op jit(solution)/shard_map/reduce_scatter | solution.py:32
  423.1 17.0 %all_gather.17 = f32[2048,16]{0,1:T(8,128)S(1)} all-gather(f32[128,16]{0,1:T(8,128)} %reduce-scatter.7.cloned.1.call-done), channel_id=1, replica_groups=mesh['row'=32,'col'=16] {'col'}, dimensions={0}, use_global_device_ids=true | all-gather | bytes 139264 | tf_op jit(solution)/shard_map/all_gather | solution.py:35
  440.1 64.7 %all-gather.9.cloned.1.call-done = f32[128,2048]{0,1:T(8,128)} async-done(((f32[128,64]{0,1:T(8,128)}), f32[128,2048]{0,1:T(8,128)}) %all-gather.9.cloned.1.call-update) | async-done | bytes 1048592 | tf_op jit(solution)/shard_map/all_gather | solution.py:20
  504.8 220.9 %reduce-scatter.9.cloned.1.call-done = f32[128,16]{0,1:T(8,128)} async-done(((f32[128,512]{0,1:T(8,128)}), f32[128,16]{0,1:T(8,128)}) %reduce-scatter.9.cloned.1.call-update) | async-done | bytes 8208 | tf_op jit(solution)/shard_map/reduce_scatter | solution.py:36
  725.7 1.8 fusion
  727.5 82.6 %all-gather.11.cloned.1.call-done = f32[2048,128]{1,0:T(8,128)} async-done(((f32[64,128]{1,0:T(8,128)}), f32[2048,128]{1,0:T(8,128)}) %all-gather.11.cloned.1.call-update) | async-done | bytes 1048592 | tf_op jit(solution)/shard_map/all_gather | solution.py:19
  810.1 2.8 convolution_bitcast_fusion
  813.0 58.9 %reduce-scatter.11.cloned.1.call-done = f32[128,16]{0,1:T(8,128)} async-done(((f32[2048,16]{0,1:T(8,128)}), f32[128,16]{0,1:T(8,128)}) %reduce-scatter.11.cloned.1.call-update) | async-done | bytes 8208 | tf_op jit(solution)/shard_map/reduce_scatter | solution.py:41
  (14 shorter events, 0.2 us)
Async XLA Ops:
  7.2 52.4 %copy-start = (f32[128,1536]{1,0:T(8,128)S(1)}, f32[128,1536]{1,0:T(8,128)}, u32[]{:S(2)}) copy-start(f32[128,1536]{1,0:T(8,128)} %param.9) | copy-start | bytes 2359300
  7.2 353.0 %copy-start.2 = (f32[128,16]{0,1:T(8,128)S(1)}, f32[128,16]{0,1:T(8,128)}, u32[]{:S(2)}) copy-start(f32[128,16]{0,1:T(8,128)} %param.14) | copy-start | bytes 24580
  7.2 356.5 %copy-start.1 = (f32[128,1536]{1,0:T(8,128)S(1)}, f32[128,1536]{1,0:T(8,128)}, u32[]{:S(2)}) copy-start(f32[128,1536]{1,0:T(8,128)} %param.10) | copy-start | bytes 2359300
  7.2 52.4 %all-gather.5.cloned.1.call-start = ((), (), s32[]{:S(2)}) async-start(), calls=%async_computation.4 | async-start | bytes 3342336 | tf_op jit(solution)/shard_map/all_gather | solution.py:22
  7.9 131.1 %all-gather.7.cloned.1.call-start = ((), (), s32[]{:S(2)}) async-start(), calls=%async_computation.6 | async-start | bytes 1081344 | tf_op jit(solution)/shard_map/all_gather | solution.py:18
  8.7 351.5 %reduce-scatter.5.cloned.1.call-start = ((), (), s32[]{:S(2)}) async-start(), calls=%async_computation.5 | async-start | bytes 270336 | tf_op jit(solution)/shard_map/reduce_scatter | solution.py:30
  64.8 660.9 %copy-start.3 = (f32[128,16]{0,1:T(8,128)S(1)}, f32[128,16]{0,1:T(8,128)}, u32[]{:S(2)}) copy-start(f32[128,16]{0,1:T(8,128)} %param.15) | copy-start | bytes 24580
  64.8 358.3 %reduce-scatter.7.cloned.1.call-start = ((), (), s32[]{:S(2)}) async-start(), calls=%async_computation.7 | async-start | bytes 139264 | tf_op jit(solution)/shard_map/reduce_scatter | solution.py:32
  363.1 141.7 %all-gather.9.cloned.1.call-start = ((), (), s32[]{:S(2)}) async-start(), calls=%async_computation.9 | async-start | bytes 1081344 | tf_op jit(solution)/shard_map/all_gather | solution.py:20
  363.7 362.0 %reduce-scatter.9.cloned.1.call-start = ((), (), s32[]{:S(2)}) async-start(), calls=%async_computation.8 | async-start | bytes 270336 | tf_op jit(solution)/shard_map/reduce_scatter | solution.py:36
  369.0 441.1 %all-gather.11.cloned.1.call-start = ((), (), s32[]{:S(2)}) async-start(), calls=%async_computation.10 | async-start | bytes 1081344 | tf_op jit(solution)/shard_map/all_gather | solution.py:19
  369.7 502.2 %reduce-scatter.11.cloned.1.call-start = ((), (), s32[]{:S(2)}) async-start(), calls=%async_computation.11 | async-start | bytes 139264 | tf_op jit(solution)/shard_map/reduce_scatter | solution.py:41
Sparse Core Ops, SparseCore 0:
  10.2 49.3 all-gather.4
  62.8 76.2 all-gather.6
  143.5 216.6 reduce-scatter.4
  363.6 59.4 reduce-scatter.6
  426.1 78.6 all-gather.8
  509.0 216.5 reduce-scatter.8
  729.3 80.7 all-gather.10
  813.7 58.1 reduce-scatter.10
where the time goes:
time: 880 us; the launch traced here: 879 us
  waiting for transfers between devices  829 us (94%)
  matrix products  18 us (2%)
  blocking collectives  17 us (2%)
  between operations  14.2 us (2%)
    reduce_scatter x1, waiting for transfers between devices, per_device(): lax.psum_scatter(partials[0], 'row', scatter_dimension=1, tiled=True)  221 us
    reduce_scatter x1, waiting for transfers between devices, per_device(): lax.psum_scatter(partials[1], 'row', scatter_dimension=1, tiled=True)  221 us
    all_gather x1, waiting for transfers between devices, per_device(): lax.all_gather(inverse_two, 'row', axis=0, tiled=True)  82.6 us
    all_gather x1, waiting for transfers between devices, per_device(): lax.all_gather(inverse_one, 'row', axis=0, tiled=True)  74.2 us
    all_gather x1, waiting for transfers between devices, per_device(): lax.all_gather(cross_block, 'row', axis=1, tiled=True)  64.7 us
    reduce_scatter x1, waiting for transfers between devices, per_device(): lax.psum_scatter(diagonal_terms(inv_two_cols, residual_two), 'col', scatt...  58.9 us
    reduce_scatter x1, waiting for transfers between devices, per_device(): lax.psum_scatter(diagonal_terms(inv_one_cols, residual_one), 'col', scatt...  53.3 us
    all_gather x1, waiting for transfers between devices, per_device(): column_piece = lax.all_gather(prior_solved, 'col', axis=1, tiled=True)  50.9 us
  transfers between devices with their start and end apart: 8, of which 8 were waited for; matrix products, arithmetic and copies ran while one was open for 1% of the time, Pallas kernels for 0%

commit v1 on v0

v1 whole, which is shorter than its diff:
```python
import functools

import jax
import jax.numpy as jnp
from jax import lax
from jax.experimental import pallas as pl
from jax.experimental.pallas import tpu as pltpu
from jax.sharding import PartitionSpec as P

NX, NZ, NY = 4, 8, 8
NC = 2 * NY
DEPTH = 1536
MESH = pl.DeviceIdType.MESH
F32 = jnp.float32
BF16 = jnp.bfloat16


def split(a):
    high = a.astype(BF16)
    return high, (a - high.astype(F32)).astype(BF16)


def dot3(a, b_high, b_low, contract):
    high, low = split(a)
    rows = a.shape[0]
    dims = (((1,), (contract,)), ((), ()))
    both = lax.dot_general(
        jnp.concatenate([high, low], axis=0), b_high, dims, preferred_element_type=F32
    )
    cross = lax.dot_general(high, b_low, dims, preferred_element_type=F32)
    return both[:rows] + both[rows:] + cross


def kernel(
    prior, block_one, block_two, cross, inv_one, inv_two, rhs_one, rhs_two,
    out_one, out_two,
    slab, blocks, b_high, b_low, mats, m_high, m_low, rhs,
    f_send, z_slots, x_send, x_slots, t_send, t_slots, s_own, s_full, c_send, c_slots,
    u_send, u_slots, s_out,
    load_sem, y_send, y_recv, p_send, p_recv, zr_send, zr_recv,
    f_sem, z_recv, xs_sem, x_recv, stage_send, stage_recv,
):
    row, col = lax.axis_index("row"), lax.axis_index("col")
    x, z = row // NZ, row % NZ
    y, core = col // 2, col % 2
    own_x = col // 4

    def at(xx, zz, cc):
        return (NZ * xx + zz, cc)

    barrier = pltpu.get_barrier_semaphore()

    def greet(device):
        pl.semaphore_signal(barrier, inc=1, device_id=device, device_id_type=MESH)

    for d in range(1, NC):
        greet(at(x, z, (col + d) % NC))
    for d in range(1, NZ):
        greet(at(x, (z + d) % NZ, col))
    for d in range(1, NX):
        greet(at((x + d) % NX, z, col))
    is_own = own_x == x
    for c in range(NC):
        @pl.when(jnp.logical_not(jnp.logical_and(is_own, col == c)))
        def _():
            greet(at(own_x, z, c))

    loads = [
        pltpu.make_async_copy(block_one, blocks.at[0], load_sem.at[0]),
        pltpu.make_async_copy(block_two, blocks.at[1], load_sem.at[1]),
        pltpu.make_async_copy(prior.at[pl.ds(0, 16)], slab.at[0, 0, 0], load_sem.at[2]),
        pltpu.make_async_copy(prior.at[pl.ds(16, 16)], slab.at[0, 0, 1], load_sem.at[3]),
        pltpu.make_async_copy(inv_one, mats.at[z, 0], load_sem.at[4]),
        pltpu.make_async_copy(inv_two, mats.at[z, 1], load_sem.at[5]),
        pltpu.make_async_copy(cross, mats.at[z, 2], load_sem.at[6]),
        pltpu.make_async_copy(rhs_one, rhs.at[0], load_sem.at[7]),
        pltpu.make_async_copy(rhs_two, rhs.at[1], load_sem.at[8]),
    ]
    for i in (2, 3, 4, 5, 6, 0, 1, 7, 8):
        loads[i].start()

    pl.semaphore_wait(
        barrier, (NC - 1) + (NZ - 1) + (NX - 1) + NC - is_own.astype(jnp.int32)
    )

    up, down = at(x, z, (col + 2) % NC), at(x, z, (col + NC - 2) % NC)
    mate = at(x, z, 2 * y + 1 - core)

    def remote(src, dst, send, recv, device):
        return pltpu.make_async_remote_copy(
            src_ref=src, dst_ref=dst, send_sem=send, recv_sem=recv,
            device_id=device, device_id_type=MESH,
        )

    def place(way, j):
        step = j // 2 + 1
        half = j % 2 if way == 0 else 1 - j % 2
        slot = 7 if step == 4 else (step if way == 0 else 3 + step)
        return slot, half

    ring = {}
    for way, device in ((0, up), (1, down)):
        for j in range(7):
            slot, half = place(way, j)
            if j < 2:
                src = prior.at[pl.ds(16 * half, 16)]
            else:
                before, same = place(way, j - 2)
                src = slab.at[0, before, half]
            ring[way, j] = remote(
                src, slab.at[0, slot, half], y_send.at[way, j], y_recv.at[way, j], device
            )
    for j in range(2):
        for way in range(2):
            ring[way, j].start()

    hand = {}
    for half in range(2):
        hand[half, -1] = remote(
            prior.at[pl.ds(16 * half, 16)], slab.at[1, 0, half],
            p_send.at[half, 7], p_recv.at[half, 7], mate,
        )
        hand[half, -1].start()
    for way in range(2):
        for j in range(7):
            slot, half = place(way, j)
            hand[way, j] = remote(
                slab.at[0, slot, half], slab.at[1, slot, half],
                p_send.at[way, j], p_recv.at[way, j], mate,
            )

    z_up, z_down = at(x, (z + 1) % NZ, col), at(x, (z + NZ - 1) % NZ, col)
    z_ring = {}
    for way, device, steps in ((0, z_up, 4), (1, z_down, 3)):
        for step in range(1, steps + 1):
            owner = (z - (step - 1) + NZ) % NZ if way == 0 else (z + step - 1) % NZ
            z_ring[way, step] = remote(
                mats.at[owner], mats.at[owner],
                zr_send.at[way, step - 1], zr_recv.at[way, step - 1], device,
            )

    def z_wait(way, step):
        owner = (z - step + NZ) % NZ if way == 0 else (z + step) % NZ
        pltpu.make_async_copy(
            mats.at[owner], mats.at[owner], zr_recv.at[way, step - 1]
        ).wait()

    for i in (4, 5, 6):
        loads[i].wait()
    for way in range(2):
        z_ring[way, 1].start()

    for b in range(2):
        loads[b].wait()
        for r in range(0, 128, 32):
            high, low = split(blocks[b, r:r + 32, :])
            b_high[128 * b + r:128 * b + r + 32, :] = high
            b_low[128 * b + r:128 * b + r + 32, :] = low
    for i in (2, 3, 7, 8):
        loads[i].wait()

    def product(j, pieces):
        a = jnp.concatenate([slab[b, s, h] for b, s, h, _, _ in pieces], axis=0)
        f = dot3(a, b_high[...], b_low[...], 1)
        for i, (_, _, half, py, pcore) in enumerate(pieces):
            index = 4 * (j + 1) + i
            f_send[index] = f[16 * i:16 * i + 16, :]
            owner_z = 4 * (py % 2) + 2 * pcore + half
            owner_x = py // 2

            @pl.when(owner_z == z)
            def _():
                z_slots[owner_x, 0] = f_send[index]

            @pl.when(owner_z != z)
            def _():
                remote(
                    f_send.at[index], z_slots.at[owner_x, (z - owner_z + NZ) % NZ],
                    f_sem.at[index], z_recv.at[owner_x], at(x, owner_z, col),
                ).start()

    def product_done(j, pieces):
        for i, (_, _, half, py, pcore) in enumerate(pieces):
            index = 4 * (j + 1) + i
            owner_z = 4 * (py % 2) + 2 * pcore + half

            @pl.when(owner_z != z)
            def _():
                pltpu.make_async_copy(
                    f_send.at[index], f_send.at[index], f_sem.at[index]
                ).wait()

    def pieces_of(j):
        if j < 0:
            return [
                (0, 0, 0, y, core), (0, 0, 1, y, core),
                (1, 0, 0, y, 1 - core), (1, 0, 1, y, 1 - core),
            ]
        step = j // 2 + 1
        low_y, high_y = (y + NY - step) % NY, (y + step) % NY
        (s0, h0), (s1, h1) = place(0, j), place(1, j)
        return [
            (0, s0, h0, low_y, core), (0, s1, h1, high_y, core),
            (1, s0, h0, low_y, 1 - core), (1, s1, h1, high_y, 1 - core),
        ]

    odd = jnp.where(y % 2 == z // 4, 0, 1)

    def over_x(q):
        shift = (0 + odd, 2 - 3 * odd, -2 + 5 * odd, 4 - 7 * odd)[q]
        which = ((y + shift + NY) % NY) // 2
        pltpu.make_async_copy(
            z_slots.at[which, pl.ds(1, NZ - 1)], z_slots.at[which, pl.ds(1, NZ - 1)],
            z_recv.at[which],
        ).wait()
        total = z_slots[which, 0]
        for d in range(1, NZ):
            total = total + z_slots[which, d]
        mine = jnp.where(which == x, 1.0, 0.0).astype(F32)
        part = jnp.concatenate([rhs[0], rhs[1]], axis=1) * mine - total
        x_slots[which, 0] = part
        x_send[q] = part
        for d in range(1, NX):
            remote(
                x_send.at[q], x_slots.at[which, NX - d],
                xs_sem.at[q, d - 1], x_recv.at[which], at((x + d) % NX, z, col),
            ).start()

    def over_x_done(q):
        for d in range(1, NX):
            pltpu.make_async_copy(x_send.at[q], x_send.at[q], xs_sem.at[q, d - 1]).wait()

    for half in range(2):
        hand[half, -1].wait_recv()
    product(-1, pieces_of(-1))
    for j in range(7):
        for way in range(2):
            ring[way, j].wait_recv()
            if j + 2 < 7:
                ring[way, j + 2].start()
            hand[way, j].start()
        if j < 4:
            z_wait(0, j + 1)
            if j + 2 <= 4:
                z_ring[0, j + 2].start()
            if j < 3:
                z_wait(1, j + 1)
                if j + 2 <= 3:
                    z_ring[1, j + 2].start()
        for way in range(2):
            hand[way, j].wait_recv()
        product(j, pieces_of(j))
        if j == 4:
            over_x(0)
            over_x(1)
            for k in range(3):
                high, low = split(mats[:, k].reshape(512, 128))
                m_high[k] = high
                m_low[k] = low
    over_x(2)
    over_x(3)

    rows = []
    for k in range(NX):
        pltpu.make_async_copy(
            x_slots.at[k, pl.ds(1, NX - 1)], x_slots.at[k, pl.ds(1, NX - 1)], x_recv.at[k]
        ).wait()
        rows.append(x_slots[k, 0] + x_slots[k, 1] + x_slots[k, 2] + x_slots[k, 3])
    residual = jnp.concatenate(rows, axis=0)

    terms = dot3(residual[:, :128], m_high[0], m_low[0], 1)
    for k in range(NX):
        for h in range(4):
            t_send[4 * k + h] = terms[16 * k:16 * k + 16, 128 * h:128 * h + 128]
    sends = []
    for d in range(1, NC):
        other = (col + d) % NC
        copy = remote(
            t_send.at[other], t_slots.at[NC - d - 1], stage_send.at[0, d], stage_recv.at[0],
            at(x, z, other),
        )
        copy.start()
        sends.append(copy)
    pltpu.make_async_copy(t_slots, t_slots, stage_recv.at[0]).wait()
    total = t_send[col]
    for d in range(NC - 1):
        total = total + t_slots[d]
    s_own[...] = total
    s_full[col] = total
    for d in range(1, NC):
        other = (col + d) % NC
        copy = remote(
            s_own, s_full.at[col], stage_send.at[1, d], stage_recv.at[1], at(x, z, other)
        )
        copy.start()
        sends.append(copy)
    swap = remote(
        s_own, s_out, stage_send.at[1, 0], stage_recv.at[4], at(own_x, z, 4 * x + col % 4)
    )

    @pl.when(is_own)
    def _():
        out_one[...] = s_own[...]

    @pl.when(jnp.logical_not(is_own))
    def _():
        swap.start()

    pltpu.make_async_copy(t_slots, t_slots, stage_recv.at[1]).wait()

    solved = jnp.concatenate(
        [
            jnp.concatenate([s_full[4 * k + h] for h in range(4)], axis=1)
            for k in range(NX)
        ],
        axis=0,
    )
    coupled = dot3(solved, m_high[2], m_low[2], 0)
    c_send[...] = coupled
    for d in range(1, NX):
        copy = remote(
            c_send, c_slots.at[NX - d - 1], stage_send.at[2, d], stage_recv.at[2],
            at((x + d) % NX, z, col),
        )
        copy.start()
        sends.append(copy)
    pltpu.make_async_copy(c_slots, c_slots, stage_recv.at[2]).wait()
    second = residual[:, 128:] - coupled - c_slots[0] - c_slots[1] - c_slots[2]

    terms = dot3(second, m_high[1], m_low[1], 1)
    for k in range(NX):
        for h in range(4):
            index = 4 * k + h
            u_send[index] = terms[16 * k:16 * k + 16, 128 * h:128 * h + 128]
            mine = jnp.logical_and(x == k, col == 4 * x + h)

            @pl.when(mine)
            def _():
                pltpu.make_async_copy(
                    u_send.at[index], u_slots.at[col], stage_recv.at[3]
                ).start()

            @pl.when(jnp.logical_not(mine))
            def _():
                remote(
                    u_send.at[index], u_slots.at[col], stage_send.at[3, index],
                    stage_recv.at[3], at(k, z, 4 * x + h),
                ).start()

    pltpu.make_async_copy(u_slots, u_slots, stage_recv.at[3]).wait()
    total = u_slots[0]
    for d in range(1, NC):
        total = total + u_slots[d]
    out_two[...] = total

    @pl.when(jnp.logical_not(is_own))
    def _():
        swap.wait()
        out_one[...] = s_out[...]

    for j in range(7):
        for way in range(2):
            ring[way, j].wait_send()
            hand[way, j].wait_send()
    for half in range(2):
        hand[half, -1].wait_send()
    for copy in z_ring.values():
        copy.wait_send()
    for j in range(-1, 7):
        product_done(j, pieces_of(j))
    for q in range(4):
        over_x_done(q)
    for copy in sends:
        copy.wait_send()
    for k in range(NX):
        for h in range(4):
            index = 4 * k + h

            @pl.when(jnp.logical_not(jnp.logical_and(x == k, col == 4 * x + h)))
            def _():
                pltpu.make_async_copy(
                    u_send.at[index], u_send.at[index], stage_send.at[3, index]
                ).wait()


def per_device(
    prior_solved, block_one, block_two, cross_block, inverse_one, inverse_two, rhs_one, rhs_two
):
    vmem = pltpu.VMEM
    dma = pltpu.SemaphoreType.DMA
    out = jax.ShapeDtypeStruct((16, 128), F32)
    one, two = pl.pallas_call(
        kernel,
        out_shape=(out, out),
        in_specs=[pl.BlockSpec(memory_space=pl.ANY)] * 8,
        out_specs=(pl.BlockSpec(memory_space=pltpu.VMEM),) * 2,
        scratch_shapes=[
            vmem((2, 8, 2, 16, DEPTH), F32),
            vmem((2, 128, DEPTH), F32),
            vmem((256, DEPTH), BF16),
            vmem((256, DEPTH), BF16),
            vmem((NZ, 3, 64, 128), F32),
            vmem((3, 512, 128), BF16),
            vmem((3, 512, 128), BF16),
            vmem((2, 16, 128), F32),
            vmem((32, 16, 256), F32),
            vmem((NX, NZ, 16, 256), F32),
            vmem((4, 16, 256), F32),
            vmem((NX, NX, 16, 256), F32),
            vmem((NC, 16, 128), F32),
            vmem((NC - 1, 16, 128), F32),
            vmem((16, 128), F32),
            vmem((NC, 16, 128), F32),
            vmem((64, 128), F32),
            vmem((NX - 1, 64, 128), F32),
            vmem((NC, 16, 128), F32),
            vmem((NC, 16, 128), F32),
            vmem((16, 128), F32),
            dma((9,)),
            dma((2, 7)),
            dma((2, 7)),
            dma((2, 8)),
            dma((2, 8)),
            dma((2, 4)),
            dma((2, 4)),
            dma((32,)),
            dma((NX,)),
            dma((4, 3)),
            dma((NX,)),
            dma((4, NC)),
            dma((5,)),
        ],
        compiler_params=pltpu.CompilerParams(
            collective_id=0, has_side_effects=True, vmem_limit_bytes=40 * 1024 * 1024
        ),
    )(
        prior_solved.T, block_one, block_two, cross_block.T, inverse_one, inverse_two,
        rhs_one.T, rhs_two.T,
    )
    return one.T, two.T


def solution(mesh):
    placed = (
        P("row", "col"),
        P("col", "row"),
        P("col", "row"),
        P("col", "row"),
        P("row", "col"),
        P("row", "col"),
        P("col", "row"),
        P("col", "row"),
    )
    return jax.shard_map(
        per_device,
        mesh=mesh,
        in_specs=placed,
        out_specs=(P("col", "row"), P("col", "row")),
        check_vma=False,
    )
```

time: 880 us -> 88.6 us (0.10)
  waiting for transfers between devices: 829 us -> 0 us
  Pallas kernels: 0 us -> 78.4 us
  matrix products: 18 us -> 0 us
  blocking collectives: 17 us -> 0 us
  between operations: 14.2 us -> 0.66 us
    reduce_scatter x4 -> x0, waiting for transfers between devices: 554 us -> none  [the longest x1 221 us: per_device(): lax.psum_scatter(partials[0], 'row', scatter_dimension=1, tiled=True)]
    all_gather x4 -> x0, waiting for transfers between devices: 272 us -> none  [the longest x1 82.6 us: per_device(): lax.all_gather(inverse_two, 'row', axis=0, tiled=True)]
    pallas_call x0 -> x1, Pallas kernels: none -> 78.4 us  [per_device(): pl.pallas_call(kernel, out_shape=(out, out), in_specs=[pl.BlockSpec(memor...]
    dot_general x5 -> x0, matrix products: 18 us -> none  [the longest x2 5.73 us: diagonal_terms(): jnp.dot(inverse_cols, residual, precision=lax.Precision.HIGHEST, preferre...]
    all_gather x1 -> x0, blocking collectives: 17 us -> none  [per_device(): solved_full = lax.all_gather(solved_one, 'col', axis=0, tiled=True)]
  transfers between devices with their start and end apart: 8 -> 0, of which waited for: 8 -> 0; matrix products, arithmetic and copies ran while one was open for 1% -> 0% of each run, Pallas kernels for 0% -> 0%
where the time goes in v1:
time: 88.6 us; the launch traced here: 87.1 us
  Pallas kernels  78.4 us (88%)
  local copies, waits for them, and re-layouts  8.05 us (9%)
    pallas_call x1, Pallas kernels, per_device(): pl.pallas_call(kernel, out_shape=(out, out), in_specs=[pl.BlockSpec(memor...  78.4 us
    unnamed x18, local copies, waits for them, and re-layouts  8.05 us

profile of v1, /device:TPU:1, one launch (start us, length us, event | category | flops | bytes accessed | tf_op | source)
XLA Modules:
  0.0 87.1 jit_solution(8500376952074519078)
XLA Ops:
  0.6 0.0 copy-start
  0.6 1.1 %copy-done = f32[128,1536]{1,0:T(8,128)S(1)} copy-done((f32[128,1536]{1,0:T(8,128)S(1)}, f32[128,1536]{1,0:T(8,128)}, u32[]{:S(2)}) %copy-start) | copy-done | bytes 786456
  1.8 0.0 copy-start.1
  1.8 1.1 %copy-done.1 = f32[128,1536]{1,0:T(8,128)S(1)} copy-done((f32[128,1536]{1,0:T(8,128)S(1)}, f32[128,1536]{1,0:T(8,128)}, u32[]{:S(2)}) %copy-start.1) | copy-done | bytes 786456
  2.9 0.0 copy-start.2
  2.9 0.9 %copy-done.2 = f32[1536,32]{0,1:T(8,128)S(1)} copy-done((f32[1536,32]{0,1:T(8,128)S(1)}, f32[1536,32]{0,1:T(8,128)}, u32[]{:S(2)}) %copy-start.2) | copy-done | bytes 196632
  3.8 0.0 copy-start.3
  3.8 0.8 copy-done.3
  4.6 0.0 copy-start.4
  4.6 0.8 copy-done.4
  5.3 0.0 copy-start.5
  5.3 0.8 copy-done.5
  6.1 0.0 copy-start.6
  6.1 0.7 copy-done.6
  6.8 0.0 copy-start.7
  6.8 0.7 copy-done.7
  7.5 78.4 %shard_map.95 = (f32[16,128]{1,0:T(8,128)S(1)}, f32[16,128]{1,0:T(8,128)S(1)}) custom-call(f32[32,1536]{1,0:T(8,128)S(1)} %bitcast.6, f32[128,1536]{1,0:T(8,128)S(1)} %copy-done, f32[128,1536]{1,0:T(8,128)S(1)} %copy-done.1, f32[64,128]{1,0:T(8,128)S(1)} %bitcast.7, f32[64,128]{1,0:T(8,128)S(1)} %copy-done.4, f32[64,128]{1,0:T(8,128)S(1)} %copy-done.5, ...), custom_call_target="tpu_custom_call" | custom-call | tf_op jit(solution)/shard_map/pallas_call | solution.py:392
  85.9 0.6 copy.12
  86.5 0.6 copy.13
Async XLA Ops:
  0.6 1.1 %copy-start = (f32[128,1536]{1,0:T(8,128)S(1)}, f32[128,1536]{1,0:T(8,128)}, u32[]{:S(2)}) copy-start(f32[128,1536]{1,0:T(8,128)} %block_one.1) | copy-start | bytes 2359300
  1.8 1.1 %copy-start.1 = (f32[128,1536]{1,0:T(8,128)S(1)}, f32[128,1536]{1,0:T(8,128)}, u32[]{:S(2)}) copy-start(f32[128,1536]{1,0:T(8,128)} %block_two.1) | copy-start | bytes 2359300
  2.9 0.9 %copy-start.2 = (f32[1536,32]{0,1:T(8,128)S(1)}, f32[1536,32]{0,1:T(8,128)}, u32[]{:S(2)}) copy-start(f32[1536,32]{0,1:T(8,128)} %param.8) | copy-start | bytes 589828
  3.8 0.8 copy-start.3
  4.6 0.8 copy-start.4
  5.3 0.8 copy-start.5
  6.1 0.7 copy-start.6
  6.8 0.7 copy-start.7

commit v2 on v0

v2 whole, which is shorter than its diff:
```python
import functools

import jax
import jax.numpy as jnp
from jax import lax
from jax.experimental import pallas as pl
from jax.experimental.pallas import tpu as pltpu
from jax.sharding import PartitionSpec as P

NX, NZ, NY = 4, 8, 8
Z_AT = (1, 4, 6)
DEPTH = 1536
MESH = pl.DeviceIdType.MESH
F32 = jnp.float32
BF16 = jnp.bfloat16


def split(a):
    high = a.astype(BF16)
    return high, (a - high.astype(F32)).astype(BF16)


def dot_split(a, b_high, b_low, contract):
    high = a.astype(BF16).astype(F32)
    both = jnp.concatenate([high, a - high], axis=0).astype(BF16)
    dims = (((1,), (contract,)), ((), ()))
    total = lax.dot_general(both, b_high, dims, preferred_element_type=F32)
    total = total + lax.dot_general(both, b_low, dims, preferred_element_type=F32)
    rows = a.shape[0]
    return total[:rows] + total[rows:]


def kernel(
    prior, block_one, block_two, cross, inv_one, inv_two, rhs_one, rhs_two,
    out_one, out_two,
    slab, blocks, b_high, b_low, mats, one_high, one_low, m_high, m_low, rhs,
    f_send, z_slots, x_send, x_slots, t_send, t_slots, s_own, s_full, s_mate, u_send, u_slots,
    load_sem, y_send, y_recv, mate_send, mate_recv, zr_send, zr_recv, zd_send, zd_recv, xr_send, xr_recv,
    f_sem, z_recv, x_sem, x_recv, stage_send, stage_recv,
):
    row, col = lax.axis_index("row"), lax.axis_index("col")
    x, z = row // NZ, row % NZ
    y, core = col // 2, col % 2
    other = 1 - core

    def at(xx, zz, yy, cc):
        return (NZ * xx + zz, 2 * yy + cc)

    def copy(src, dst, sem):
        return pltpu.make_async_copy(src, dst, sem)

    def remote(src, dst, send, recv, device):
        return pltpu.make_async_remote_copy(
            src_ref=src, dst_ref=dst, send_sem=send, recv_sem=recv,
            device_id=device, device_id_type=MESH,
        )

    def arrived(ref, sem):
        copy(ref, ref, sem).wait()

    own_half = slice(None)
    loads = [
        copy(inv_one, mats.at[core, 0, x, z], load_sem.at[0]),
        copy(cross, mats.at[core, 1, x, z], load_sem.at[1]),
        copy(inv_two, mats.at[core, 2, x, z], load_sem.at[2]),
        copy(block_one, blocks.at[core, pl.ds(0, 128)], load_sem.at[3]),
        copy(block_two, blocks.at[core, pl.ds(128, 128)], load_sem.at[4]),
        copy(prior.at[pl.ds(0, 16)], slab.at[7, 0], load_sem.at[5]),
        copy(prior.at[pl.ds(16, 16)], slab.at[7, 1], load_sem.at[6]),
        copy(rhs_one.at[pl.ds(pl.multiple_of(8 * core, 8), 8)], rhs.at[core, 0], load_sem.at[7]),
        copy(rhs_two.at[pl.ds(pl.multiple_of(8 * core, 8), 8)], rhs.at[core, 1], load_sem.at[8]),
    ]
    for load in loads:
        load.start()

    barrier = pltpu.get_barrier_semaphore()

    def greet(device):
        pl.semaphore_signal(barrier, inc=1, device_id=device, device_id_type=MESH)

    for d in (2, 14, 1, 4, 12, 3, 13, 5, 11, 6, 10, 7, 9, 8, 15):
        greet((row, (col + d) % 16))
    for d in range(1, NZ):
        greet(at(x, (z + d) % NZ, y, core))
    for d in range(1, NX):
        greet(at((x + d) % NX, z, y, core))
    maker = (z // 2) % 2

    @pl.when(maker != core)
    def _():
        for d in range(NZ):
            greet(at(x, (z + d) % NZ, y, maker))

    own_x = y // 2

    @pl.when(own_x != x)
    def _():
        for d in range(NY):
            greet(at(own_x, z, (y + d) % NY, core))

    pl.semaphore_wait(barrier, 15 + 7 + 3 + 4 + 6)
    makes_own = maker == core
    sums_own = own_x == x

    def half_of(way, i):
        return i % 2 if way == 0 else 1 - i % 2

    neighbours = (at(x, z, (y + 1) % NY, core), at(x, z, (y + NY - 1) % NY, core))
    ring = {}
    for way in range(2):
        for j in range(14):
            i, sub = j // 2, j % 2
            if i < 2:
                src = prior.at[pl.ds(16 * half_of(way, i) + 8 * sub, 8)]
            else:
                src = slab.at[i - 2, way, pl.ds(8 * sub, 8)]
            ring[way, j] = remote(
                src, slab.at[i, way, pl.ds(8 * sub, 8)],
                y_send, y_recv.at[way, j], neighbours[way],
            )
    for j in range(4):
        for way in range(2):
            ring[way, j].start()

    mate = at(x, z, y, other)
    other_rows = pl.ds(pl.multiple_of(8 * other, 8), 8)
    hands = [
        remote(block_one, blocks.at[core, pl.ds(0, 128)], mate_send.at[0], mate_recv.at[0], mate),
        remote(block_two, blocks.at[core, pl.ds(128, 128)], mate_send.at[1], mate_recv.at[1], mate),
        remote(rhs_one.at[other_rows], rhs.at[core, 0], mate_send.at[2], mate_recv.at[2], mate),
        remote(rhs_two.at[other_rows], rhs.at[core, 1], mate_send.at[3], mate_recv.at[3], mate),
    ]
    for hand in hands:
        hand.start()

    z_next = (at(x, (z + 1) % NZ, y, core), at(x, (z + NZ - 1) % NZ, y, core))
    order = (2, 0)

    def z_owner(way, step):
        return (z + NZ - step) % NZ if way == 0 else (z + step) % NZ

    def z_start(way, k, step):
        ref = mats.at[core, k, x, z_owner(way, step - 1)]
        remote(ref, ref, zr_send, zr_recv.at[way, k, step - 1], z_next[way]).start()

    def z_step(step):
        for k in order:
            for way in range(2):
                if step > (4, 3)[way]:
                    continue
                arrived(mats.at[core, k, x, z_owner(way, step)], zr_recv.at[way, k, step - 1])
                if step < (4, 3)[way]:
                    z_start(way, k, step + 1)

    x_next = (at((x + 1) % NX, z, y, core), at((x + 3) % NX, z, y, core))
    x_before = ((x + 3) % NX, (x + 1) % NX)

    def x_start(k):
        for way in range(2):
            ref = mats.at[core, k, x]
            remote(
                ref, ref, xr_send.at[k - 1, way, 0], xr_recv.at[k - 1, way, 0], x_next[way]
            ).start()

    def x_forward(k):
        for way in range(2):
            arrived(mats.at[core, k, x_before[way]], xr_recv.at[k - 1, way, 0])
            ref = mats.at[core, k, x_before[way], pl.ds(4 * way, 4)]
            remote(
                ref, ref, xr_send.at[k - 1, way, 1], xr_recv.at[k - 1, way, 1], x_next[way]
            ).start()

    def x_end(k):
        for way in range(2):
            arrived(mats.at[core, k, (x + 2) % NX, pl.ds(4 * way, 4)], xr_recv.at[k - 1, way, 1])
        remote(
            mats.at[core, k], mats.at[core, k], mate_send.at[4 + k], mate_recv.at[4 + k], mate
        ).start()

    def panel(k):
        arrived(mats.at[other, k], mate_recv.at[4 + k])
        for xx in range(NX):
            both = jnp.concatenate(
                [mats[c, k, xx].reshape(512, 128) for c in range(2)], axis=1
            )
            high, low = split(both)
            m_high[k - 1, 512 * xx:512 * xx + 512, :] = high
            m_low[k - 1, 512 * xx:512 * xx + 512, :] = low

    loads[1].wait()
    for d in (4, 3, 5, 2, 6, 1, 7):
        ref = mats.at[core, 1, x, z]
        remote(ref, ref, zd_send, zd_recv, at(x, (z + d) % NZ, y, core)).start()
    for k in order:
        loads[k].wait()
        for way in range(2):
            z_start(way, k, 1)

    def halves(c):
        for r in range(0, 256, 32):
            high, low = split(blocks[c, r:r + 32, :])
            b_high[c, r:r + 32, :] = high
            b_low[c, r:r + 32, :] = low

    def owner_of(i, way):
        if i == 7:
            py, half = y, way
        else:
            step = i // 2 + 1
            py = (y + NY - step) % NY if way == 0 else (y + step) % NY
            half = half_of(way, i)
        return py // 2, 4 * (py % 2) + 2 * core + half

    def product(i):
        a = slab[i].reshape(32, DEPTH)
        f = dot_split(
            a, b_high[...].reshape(512, DEPTH), b_low[...].reshape(512, DEPTH), 1
        )
        for way in range(2):
            owner_x, owner_z = owner_of(i, way)
            slot = z_slots.at[owner_x, (z - owner_z + NZ) % NZ]
            for c in range(2):
                index = 4 * i + 2 * way + c
                r = 16 * way + 8 * c
                f_send[index] = f[r:r + 8, :]
                mine = jnp.logical_and(owner_z == z, core == c)

                @pl.when(mine)
                def _():
                    copy(f_send.at[index], slot, z_recv.at[owner_x]).start()

                @pl.when(jnp.logical_not(mine))
                def _():
                    remote(
                        f_send.at[index], slot, f_sem, z_recv.at[owner_x],
                        at(x, owner_z, y, c),
                    ).start()

    odd = jnp.where(y % 2 == z // 4, 0, 1)

    def over_x(q):
        shift = (0 + odd, 2 - 3 * odd, -2 + 5 * odd, 4 - 7 * odd)[q]
        which = ((y + shift + NY) % NY) // 2
        arrived(z_slots.at[which], z_recv.at[which])
        total = z_slots[which, 0]
        for d in range(1, NZ):
            total = total + z_slots[which, d]
        mine = jnp.where(which == x, 1.0, 0.0).astype(F32)
        given = jnp.concatenate([rhs[0, 0], rhs[0, 1], rhs[1, 0], rhs[1, 1]], axis=1)
        part = given * mine - total
        x_slots[which, 0] = part
        x_send[q] = part
        for d in (2, 1, 3):
            remote(
                x_send.at[q], x_slots.at[which, NX - d], x_sem, x_recv,
                at((x + d) % NX, z, y, core),
            ).start()

    for i in range(7):
        for sub in range(2):
            j = 2 * i + sub
            for way in range(2):
                ring[way, j].wait_recv()
                if j + 4 < 14:
                    ring[way, j + 4].start()
            if j == 0:
                for load in loads[3:]:
                    load.wait()
                halves(core)
            if j == 1:
                for hand in hands[:2]:
                    hand.wait_recv()
                halves(other)
            if j == 2:
                product(7)
            if j == 3:
                product(0)
            if sub == 0 and i >= 2:
                product(i - 1)
        if i in Z_AT:
            z_step(Z_AT.index(i) + 1)
        if i == 3:
            arrived(mats.at[core, 1, x, pl.ds(0, 7)], zd_recv)
            x_start(1)
    product(6)
    x_forward(1)
    z_step(4)
    x_start(2)
    remote(
        mats.at[core, 0, x], mats.at[core, 0, x], mate_send.at[4], mate_recv.at[4], mate
    ).start()
    for hand in hands[2:]:
        hand.wait_recv()
    for q in range(3):
        over_x(q)
    arrived(mats.at[other, 0, x], mate_recv.at[4])
    both = jnp.concatenate([mats[c, 0, x].reshape(512, 128) for c in range(2)], axis=1)
    high, low = split(both)
    one_high[...] = high
    one_low[...] = low
    over_x(3)
    x_end(1)

    arrived(x_slots.at[pl.ds(0, 3)], x_recv)

    def residual(k):
        return x_slots[k, 0] + x_slots[k, 1] + x_slots[k, 2] + x_slots[k, 3]

    def of_block(b, r):
        return jnp.concatenate(
            [r[:, 128 * b:128 * b + 128], r[:, 256 + 128 * b:384 + 128 * b]], axis=1
        )

    first = jnp.concatenate([of_block(0, residual(k)) for k in range(NX)], axis=0)

    terms = dot_split(first, one_high[...], one_low[...], 1)
    for k in range(NX):
        for e in range(2):
            index = 2 * k + e
            t_send[index] = terms[8 * k:8 * k + 8, 256 * e:256 * e + 256]
            mine = jnp.logical_and(x == k, y == 2 * x + e)

            @pl.when(mine)
            def _():
                copy(t_send.at[index], t_slots.at[y], stage_recv.at[0]).start()

            @pl.when(jnp.logical_not(mine))
            def _():
                remote(
                    t_send.at[index], t_slots.at[y], stage_send.at[0], stage_recv.at[0],
                    at(k, z, 2 * x + e, core),
                ).start()

    x_forward(2)
    panel(1)
    second = of_block(1, residual(x))
    arrived(t_slots, stage_recv.at[0])
    total = t_slots[0]
    for d in range(1, NY):
        total = total + t_slots[d]
    s_own[...] = total
    s_full[y] = total
    for d in (4, 3, 5, 2, 6, 1, 7):
        remote(
            s_own, s_full.at[y], stage_send.at[1], stage_recv.at[1],
            at(x, z, (y + d) % NY, core),
        ).start()
    s_mate[0] = total[:, :128]
    s_mate[1] = total[:, 128:]
    swap = remote(
        s_mate.at[other], s_mate.at[2], mate_send.at[7], mate_recv.at[7], mate
    )
    swap.start()
    x_end(2)
    swap.wait()
    out_one[pl.ds(pl.multiple_of(8 * core, 8), 8), :] = s_mate[core]
    out_one[pl.ds(pl.multiple_of(8 * other, 8), 8), :] = s_mate[2]

    arrived(slab.at[pl.ds(0, 7)], y_send)
    for hand in hands:
        hand.wait_send()
    arrived(mats.at[core, 0, x], mate_send.at[4])
    arrived(mats.at[core, pl.ds(0, 2), 0, pl.ds(0, 7)], zr_send)
    arrived(mats.at[core, 0, 0, pl.ds(0, 7)], zd_send)
    for k in range(1, 3):
        for way in range(2):
            arrived(mats.at[core, k, x], xr_send.at[k - 1, way, 0])
            arrived(mats.at[core, k, x, pl.ds(0, 4)], xr_send.at[k - 1, way, 1])
        arrived(mats.at[core, k], mate_send.at[4 + k])

    @pl.when(makes_own)
    def _():
        arrived(f_send.at[pl.ds(0, 28)], f_sem)

    @pl.when(jnp.logical_not(makes_own))
    def _():
        arrived(f_send, f_sem)

    arrived(x_slots.at[pl.ds(0, 3)], x_sem)

    @pl.when(sums_own)
    def _():
        arrived(t_send.at[pl.ds(0, 7)], stage_send.at[0])

    @pl.when(jnp.logical_not(sums_own))
    def _():
        arrived(t_send, stage_send.at[0])

    panel(2)

    arrived(s_full.at[pl.ds(0, 7)], stage_recv.at[1])
    solved = jnp.concatenate([s_full[k] for k in range(NY)], axis=1)
    second = second - dot_split(solved, m_high[0], m_low[0], 0)

    terms = dot_split(second, m_high[1], m_low[1], 1)
    for k in range(16):
        u_send[k] = terms[:, 128 * k:128 * k + 128]
    u_slots[8 * core + y] = u_send[col]
    for d in (8, 9, 7, 6, 10, 5, 11, 4, 12, 3, 13, 2, 14, 1, 15):
        to = (col + d) % 16
        remote(
            u_send.at[to], u_slots.at[8 * core + y], stage_send.at[2], stage_recv.at[2],
            (row, to),
        ).start()
    arrived(s_full.at[pl.ds(0, 7)], stage_send.at[1])
    arrived(u_slots.at[pl.ds(0, 15)], stage_recv.at[2])
    for half in range(2):
        total = u_slots[8 * half]
        for d in range(1, NY):
            total = total + u_slots[8 * half + d]
        out_two[8 * half:8 * half + 8, :] = total
    arrived(u_slots.at[pl.ds(0, 15)], stage_send.at[2])


def per_device(
    prior_solved, block_one, block_two, cross_block, inverse_one, inverse_two, rhs_one, rhs_two
):
    vmem = pltpu.VMEM
    dma = pltpu.SemaphoreType.DMA
    out = jax.ShapeDtypeStruct((16, 128), F32)
    one, two = pl.pallas_call(
        kernel,
        out_shape=(out, out),
        in_specs=[pl.BlockSpec(memory_space=pltpu.HBM)] * 8,
        out_specs=(pl.BlockSpec(memory_space=pltpu.VMEM),) * 2,
        scratch_shapes=[
            vmem((8, 2, 16, DEPTH), F32),
            vmem((2, 256, DEPTH), F32),
            vmem((2, 256, DEPTH), BF16),
            vmem((2, 256, DEPTH), BF16),
            vmem((2, 3, NX, NZ, 64, 128), F32),
            vmem((512, 256), BF16),
            vmem((512, 256), BF16),
            vmem((2, 2048, 256), BF16),
            vmem((2, 2048, 256), BF16),
            vmem((2, 2, 8, 128), F32),
            vmem((32, 8, 512), F32),
            vmem((NX, NZ, 8, 512), F32),
            vmem((4, 8, 512), F32),
            vmem((NX, NX, 8, 512), F32),
            vmem((8, 8, 256), F32),
            vmem((NY, 8, 256), F32),
            vmem((8, 256), F32),
            vmem((NY, 8, 256), F32),
            vmem((3, 8, 128), F32),
            vmem((16, 8, 128), F32),
            vmem((16, 8, 128), F32),
            dma((9,)),
            dma,
            dma((2, 14)),
            dma((8,)),
            dma((8,)),
            dma,
            dma((2, 3, 4)),
            dma,
            dma,
            dma((2, 2, 2)),
            dma((2, 2, 2)),
            dma,
            dma((NX,)),
            dma,
            dma,
            dma((3,)),
            dma((3,)),
        ],
        compiler_params=pltpu.CompilerParams(
            collective_id=0, has_side_effects=True, vmem_limit_bytes=62 * 1024 * 1024
        ),
    )(
        prior_solved.T, block_one, block_two, cross_block.T, inverse_one, inverse_two,
        rhs_one.T, rhs_two.T,
    )
    return one.T, two.T


def solution(mesh):
    placed = (
        P("row", "col"),
        P("col", "row"),
        P("col", "row"),
        P("col", "row"),
        P("row", "col"),
        P("row", "col"),
        P("col", "row"),
        P("col", "row"),
    )
    return jax.shard_map(
        per_device,
        mesh=mesh,
        in_specs=placed,
        out_specs=(P("col", "row"), P("col", "row")),
        check_vma=False,
    )
```

time: 880 us -> 73.5 us (0.08)
  waiting for transfers between devices: 829 us -> 0 us
  Pallas kernels: 0 us -> 70.8 us
  matrix products: 18 us -> 0 us
  blocking collectives: 17 us -> 0 us
  between operations: 14.2 us -> 0.65 us
    reduce_scatter x4 -> x0, waiting for transfers between devices: 554 us -> none  [the longest x1 221 us: per_device(): lax.psum_scatter(partials[0], 'row', scatter_dimension=1, tiled=True)]
    all_gather x4 -> x0, waiting for transfers between devices: 272 us -> none  [the longest x1 82.6 us: per_device(): lax.all_gather(inverse_two, 'row', axis=0, tiled=True)]
    pallas_call x0 -> x1, Pallas kernels: none -> 70.8 us  [per_device(): pl.pallas_call(kernel, out_shape=(out, out), in_specs=[pl.BlockSpec(memor...]
    dot_general x5 -> x0, matrix products: 18 us -> none  [the longest x2 5.73 us: diagonal_terms(): jnp.dot(inverse_cols, residual, precision=lax.Precision.HIGHEST, preferre...]
    all_gather x1 -> x0, blocking collectives: 17 us -> none  [per_device(): solved_full = lax.all_gather(solved_one, 'col', axis=0, tiled=True)]
  transfers between devices with their start and end apart: 8 -> 0, of which waited for: 8 -> 0; matrix products, arithmetic and copies ran while one was open for 1% -> 0% of each run, Pallas kernels for 0% -> 0%
where the time goes in v2:
time: 73.5 us; the launch traced here: 73.3 us
  Pallas kernels  70.8 us (96%)
  local copies, waits for them, and re-layouts  1.9 us (3%)
    pallas_call x1, Pallas kernels, per_device(): pl.pallas_call(kernel, out_shape=(out, out), in_specs=[pl.BlockSpec(memor...  70.8 us
    unnamed x4, local copies, waits for them, and re-layouts  1.9 us

profile of v2, /device:TPU:1, one launch (start us, length us, event | category | flops | bytes accessed | tf_op | source)
XLA Modules:
  0.0 73.3 jit_solution(10253349260313076079)
XLA Ops:
  0.6 70.8 %shard_map.95 = (f32[16,128]{1,0:T(8,128)}, f32[16,128]{1,0:T(8,128)}) custom-call(f32[32,1536]{1,0:T(8,128)} %bitcast.6, f32[128,1536]{1,0:T(8,128)} %block_one.1, f32[128,1536]{1,0:T(8,128)} %block_two.1, f32[64,128]{1,0:T(8,128)} %bitcast.7, f32[64,128]{1,0:T(8,128)} %inv_one.1, f32[64,128]{1,0:T(8,128)} %inv_two.1, f32[16,128]{1,0:T(8,128)} %bitcast.8, ...), custom_call_target="tpu_custom_call" | custom-call | tf_op jit(solution)/shard_map/pallas_call | solution.py:421
  71.4 0.0 copy-start
  71.4 1.3 %copy.12 = f32[128,16]{0,1:T(8,128)} copy(f32[128,16]{0,1:T(8,128)} %bitcast.11) | data formatting | bytes 16384
  72.7 0.0 copy-done
  72.7 0.6 copy.13
Async XLA Ops:
  71.4 1.3 %copy-start = (f32[16,128]{1,0:T(8,128)S(1)}, f32[16,128]{1,0:T(8,128)}, u32[]{:S(2)}) copy-start(f32[16,128]{1,0:T(8,128)} %get-tuple-element.5) | copy-start | bytes 24580

commit v3 on v2

v3 whole, which is shorter than its diff:
```python
import functools

import jax
import jax.numpy as jnp
from jax import lax
from jax.experimental import pallas as pl
from jax.experimental.pallas import tpu as pltpu
from jax.sharding import PartitionSpec as P

NX, NZ, NY = 4, 8, 8
C_AT = 0
X_AT = (3, 5)
RING_AT = (2, 5, 6)
DEPTH = 1536
MESH = pl.DeviceIdType.MESH
F32 = jnp.float32
BF16 = jnp.bfloat16


def split(a):
    high = a.astype(BF16)
    return high, (a - high.astype(F32)).astype(BF16)


def dot_split(a, b_high, b_low, contract):
    high = a.astype(BF16).astype(F32)
    both = jnp.concatenate([high, a - high], axis=0).astype(BF16)
    dims = (((1,), (contract,)), ((), ()))
    total = lax.dot_general(both, b_high, dims, preferred_element_type=F32)
    total = total + lax.dot_general(both, b_low, dims, preferred_element_type=F32)
    rows = a.shape[0]
    return total[:rows] + total[rows:]


def kernel(
    prior, block_one, block_two, cross, inv_one, inv_two, rhs_one, rhs_two,
    out,
    slab, blocks, b_high, b_low, mats, m_high, m_low, rhs,
    f_send, x_slots, q_send, z_slots, t_send, t_slots, s_own, s_full, s_mate, u_send, u_slots,
    load_sem, y_send, y_recv, mate_send, mate_recv, zd_send, zd_recv, xd_send, xd_recv, zr_send, zr_recv, xr_send, xr_recv,
    f_sem, f_recv, q_sem, q_recv, stage_send, stage_recv,
):
    row, col = lax.axis_index("row"), lax.axis_index("col")
    x, z = row // NZ, row % NZ
    y, core = col // 2, col % 2
    other = 1 - core

    def at(xx, zz, yy, cc):
        return (NZ * xx + zz, 2 * yy + cc)

    def copy(src, dst, sem):
        return pltpu.make_async_copy(src, dst, sem)

    def remote(src, dst, send, recv, device):
        return pltpu.make_async_remote_copy(
            src_ref=src, dst_ref=dst, send_sem=send, recv_sem=recv,
            device_id=device, device_id_type=MESH,
        )

    def arrived(ref, sem):
        copy(ref, ref, sem).wait()

    own_half = slice(None)
    loads = [
        copy(inv_one, mats.at[core, 0, x, z], load_sem.at[0]),
        copy(cross, mats.at[core, 1, x, z], load_sem.at[1]),
        copy(inv_two, mats.at[core, 2, x, z], load_sem.at[2]),
        copy(block_one, blocks.at[core, pl.ds(0, 128)], load_sem.at[3]),
        copy(block_two, blocks.at[core, pl.ds(128, 128)], load_sem.at[4]),
        copy(prior.at[pl.ds(0, 16)], slab.at[7, 0], load_sem.at[5]),
        copy(prior.at[pl.ds(16, 16)], slab.at[7, 1], load_sem.at[6]),
        copy(rhs_one.at[pl.ds(pl.multiple_of(8 * core, 8), 8)], rhs.at[core, 0], load_sem.at[7]),
        copy(rhs_two.at[pl.ds(pl.multiple_of(8 * core, 8), 8)], rhs.at[core, 1], load_sem.at[8]),
    ]
    for load in loads:
        load.start()

    barrier = pltpu.get_barrier_semaphore()

    def greet(device):
        pl.semaphore_signal(barrier, inc=1, device_id=device, device_id_type=MESH)

    for d in (2, 14, 1, 4, 12, 3, 13, 5, 11, 6, 10, 7, 9, 8, 15):
        greet((row, (col + d) % 16))
    for d in range(1, NZ):
        greet(at(x, (z + d) % NZ, y, core))
    for d in range(1, NX):
        for c in range(2):
            greet(at((x + d) % NX, z, y, c))
    pl.semaphore_wait(barrier, 15 + 7 + 6)

    def half_of(way, i):
        return i % 2 if way == 0 else 1 - i % 2

    neighbours = (at(x, z, (y + 1) % NY, core), at(x, z, (y + NY - 1) % NY, core))
    ring = {}
    for way in range(2):
        for j in range(14):
            i, sub = j // 2, j % 2
            if i < 2:
                src = prior.at[pl.ds(16 * half_of(way, i) + 8 * sub, 8)]
            else:
                src = slab.at[i - 2, way, pl.ds(8 * sub, 8)]
            ring[way, j] = remote(
                src, slab.at[i, way, pl.ds(8 * sub, 8)],
                y_send, y_recv.at[way, j], neighbours[way],
            )
    for j in range(4):
        for way in range(2):
            ring[way, j].start()

    mate = at(x, z, y, other)
    other_rows = pl.ds(pl.multiple_of(8 * other, 8), 8)
    hands = [
        remote(block_one, blocks.at[core, pl.ds(0, 128)], mate_send.at[0], mate_recv.at[0], mate),
        remote(block_two, blocks.at[core, pl.ds(128, 128)], mate_send.at[1], mate_recv.at[1], mate),
        remote(rhs_one.at[other_rows], rhs.at[core, 0], mate_send.at[2], mate_recv.at[2], mate),
        remote(rhs_two.at[other_rows], rhs.at[core, 1], mate_send.at[3], mate_recv.at[3], mate),
    ]
    for hand in hands:
        hand.start()

    def z_start(k):
        loads[k].wait()
        for d in (4, 3, 5, 2, 6, 1, 7):
            ref = mats.at[core, k, x, z]
            remote(
                ref, ref, zd_send, zd_recv.at[k], at(x, (z + d) % NZ, y, core)
            ).start()

    def z_end(k):
        arrived(mats.at[core, k, x, pl.ds(0, 7)], zd_recv.at[k])

    def two_start():
        loads[2].wait()
        ref = mats.at[core, 2, x, z]
        for d in (2, 1, 3):
            remote(ref, ref, xd_send, xd_recv, at((x + d) % NX, z, y, core)).start()

    z_next = (at(x, (z + 1) % NZ, y, core), at(x, (z + NZ - 1) % NZ, y, core))

    def two_step(step):
        if step == 0:
            arrived(mats.at[core, 2, pl.ds(0, 3), z], xd_recv)
        for way in range(2):
            last = (4, 3)[way]
            owner = (z + NZ - step) % NZ if way == 0 else (z + step) % NZ
            ref = mats.at[core, 2, pl.ds(0, NX), owner]
            if 0 < step <= last:
                arrived(ref, zr_recv.at[way, step - 1])
            if step < last:
                remote(ref, ref, zr_send, zr_recv.at[way, step], z_next[way]).start()

    x_next = (at((x + 1) % NX, z, y, core), at((x + 3) % NX, z, y, core))
    x_before = ((x + 3) % NX, (x + 1) % NX)

    def x_start(k):
        for way in range(2):
            ref = mats.at[core, k, x]
            remote(
                ref, ref, xr_send.at[k, way, 0], xr_recv.at[k, way, 0], x_next[way]
            ).start()

    def x_forward(k):
        for way in range(2):
            arrived(mats.at[core, k, x_before[way]], xr_recv.at[k, way, 0])
            ref = mats.at[core, k, x_before[way], pl.ds(4 * way, 4)]
            remote(
                ref, ref, xr_send.at[k, way, 1], xr_recv.at[k, way, 1], x_next[way]
            ).start()

    def to_mate(k):
        remote(
            mats.at[core, k], mats.at[core, k], mate_send.at[4 + k], mate_recv.at[4 + k], mate
        ).start()

    def x_end(k):
        for way in range(2):
            arrived(mats.at[core, k, (x + 2) % NX, pl.ds(4 * way, 4)], xr_recv.at[k, way, 1])
        to_mate(k)

    def panel_rows(k, xx):
        both = jnp.concatenate(
            [mats[c, k, xx].reshape(512, 128) for c in range(2)], axis=1
        )
        high, low = split(both)
        m_high[k, xx] = high
        m_low[k, xx] = low

    def panel(k):
        arrived(mats.at[other, k], mate_recv.at[4 + k])
        for xx in range(NX):
            panel_rows(k, xx)

    def one_to_mate(d, sem):
        ref = mats.at[core, 0, (x + d) % NX]
        remote(ref, ref, mate_send.at[sem], mate_recv.at[sem], mate).start()

    def one_near():
        arrived(mats.at[other, 0, pl.ds(0, 3)], mate_recv.at[4])
        for d in (0, 1, 3):
            panel_rows(0, (x + d) % NX)

    def one_far():
        for way in range(2):
            arrived(mats.at[core, 0, (x + 2) % NX, pl.ds(4 * way, 4)], xr_recv.at[0, way, 1])
        one_to_mate(2, 8)
        arrived(mats.at[other, 0, (x + 2) % NX], mate_recv.at[8])
        panel_rows(0, (x + 2) % NX)

    z_start(0)
    two_start()

    def halves(c):
        for r in range(0, 256, 32):
            high, low = split(blocks[c, r:r + 32, :])
            b_high[c, r:r + 32, :] = high
            b_low[c, r:r + 32, :] = low

    def owner_of(i, way):
        if i == 7:
            py, half = y, way
        else:
            step = i // 2 + 1
            py = (y + NY - step) % NY if way == 0 else (y + step) % NY
            half = half_of(way, i)
        return py // 2, 4 * (py % 2) + 2 * core + half

    def product(i):
        a = slab[i].reshape(32, DEPTH)
        f = dot_split(
            a, b_high[...].reshape(512, DEPTH), b_low[...].reshape(512, DEPTH), 1
        )
        for way in range(2):
            owner_x, owner_z = owner_of(i, way)
            slot = x_slots.at[owner_z, (x - owner_x + NX) % NX]
            for c in range(2):
                index = 4 * i + 2 * way + c
                r = 16 * way + 8 * c
                f_send[index] = f[r:r + 8, :]
                mine = jnp.logical_and(owner_x == x, core == c)

                @pl.when(mine)
                def _():
                    copy(f_send.at[index], slot, f_recv.at[owner_z]).start()

                @pl.when(jnp.logical_not(mine))
                def _():
                    remote(
                        f_send.at[index], slot, f_sem, f_recv.at[owner_z],
                        at(owner_x, z, y, c),
                    ).start()

    def apart(a):
        return jnp.minimum((a - y + NY) % NY, (y - a + NY) % NY)

    far = jnp.where(apart(2 * x) > apart(2 * x + 1), 0, 1)

    def over_z(which):
        arrived(x_slots.at[which], f_recv.at[which])
        total = x_slots[which, 0]
        for d in range(1, NX):
            total = total + x_slots[which, d]

        @pl.when(which == z)
        def _():
            z_slots[0] = total

        @pl.when(which != z)
        def _():
            q_send[which] = total
            remote(
                q_send.at[which], z_slots.at[(z - which + NZ) % NZ], q_sem, q_recv,
                at(x, which, y, core),
            ).start()

    for i in range(7):
        for sub in range(2):
            j = 2 * i + sub
            for way in range(2):
                ring[way, j].wait_recv()
                if j + 4 < 14:
                    ring[way, j + 4].start()
            if j == 0:
                for load in loads[3:]:
                    load.wait()
                halves(core)
            if j == 1:
                for hand in hands[:2]:
                    hand.wait_recv()
                halves(other)
            if j == 2:
                product(7)
            if j == 3:
                product(0)
            if sub == 0 and i >= 2:
                product(i - 1)
        if i == C_AT:
            z_start(1)
        if i in RING_AT:
            two_step(RING_AT.index(i))
        if i in X_AT:
            z_end(X_AT.index(i))
            x_start(X_AT.index(i))
    product(6)
    x_forward(0)
    for d in (0, 1, 3):
        one_to_mate(d, 4)
    for hand in hands[2:]:
        hand.wait_recv()
    for t in range(4):
        over_z(4 * (1 - far) + t)
    for t in range(4):
        over_z(4 * far + t)
    two_step(3)
    one_near()
    x_forward(1)
    one_far()

    arrived(z_slots.at[pl.ds(1, NZ - 1)], q_recv)
    total = z_slots[0]
    for d in range(1, NZ):
        total = total + z_slots[d]
    residual = (
        jnp.concatenate([rhs[0, 0], rhs[0, 1], rhs[1, 0], rhs[1, 1]], axis=1) - total
    )

    def weights(ref, k):
        return ref[k].reshape(2048, 256)

    def of_block(b):
        return jnp.concatenate(
            [residual[:, 128 * b:128 * b + 128], residual[:, 256 + 128 * b:384 + 128 * b]], axis=1
        )

    terms = dot_split(of_block(0), weights(m_high, 0), weights(m_low, 0), 1)
    for k in range(NY):
        t_send[k] = terms[:, 256 * k:256 * k + 256]
    for d in (4, 3, 5, 2, 6, 1, 7):
        to = (y + d) % NY
        remote(
            t_send.at[to], t_slots.at[NY - 1 - d], stage_send.at[0], stage_recv.at[0],
            at(x, z, to, core),
        ).start()

    x_end(1)
    two_step(4)
    to_mate(2)
    second = of_block(1)
    arrived(t_slots, stage_recv.at[0])
    total = t_send[y]
    for d in range(NY - 1):
        total = total + t_slots[d]
    s_own[...] = total
    s_full[y] = total
    for d in (4, 3, 5, 2, 6, 1, 7):
        remote(
            s_own, s_full.at[y], stage_send.at[1], stage_recv.at[1],
            at(x, z, (y + d) % NY, core),
        ).start()
    s_mate[0] = total[:, :128]
    s_mate[1] = total[:, 128:]
    swap = remote(
        s_mate.at[other], s_mate.at[2], mate_send.at[7], mate_recv.at[7], mate
    )
    swap.start()
    panel(1)
    swap.wait()
    out[0, pl.ds(pl.multiple_of(8 * core, 8), 8), :] = s_mate[core]
    out[0, pl.ds(pl.multiple_of(8 * other, 8), 8), :] = s_mate[2]

    arrived(slab.at[pl.ds(0, 7)], y_send)
    for hand in hands:
        hand.wait_send()
    arrived(mats.at[core, pl.ds(0, 2), 0, pl.ds(0, 7)], zd_send)
    arrived(mats.at[core, 2, pl.ds(0, 3), 0], xd_send)
    arrived(mats.at[core, 2, pl.ds(0, 4), pl.ds(0, 7)], zr_send)
    for k in range(2):
        for way in range(2):
            arrived(mats.at[core, k, x], xr_send.at[k, way, 0])
            arrived(mats.at[core, k, x, pl.ds(0, 4)], xr_send.at[k, way, 1])
    arrived(mats.at[core, 0, pl.ds(0, 3)], mate_send.at[4])
    arrived(mats.at[core, 0, 0], mate_send.at[8])
    for k in range(1, 3):
        arrived(mats.at[core, k], mate_send.at[4 + k])
    arrived(f_send.at[pl.ds(0, 28)], f_sem)
    arrived(q_send.at[pl.ds(0, 7)], q_sem)
    arrived(t_slots, stage_send.at[0])
    panel(2)

    arrived(s_full.at[pl.ds(0, 7)], stage_recv.at[1])
    solved = jnp.concatenate([s_full[k] for k in range(NY)], axis=1)
    second = second - dot_split(solved, weights(m_high, 1), weights(m_low, 1), 0)

    terms = dot_split(second, weights(m_high, 2), weights(m_low, 2), 1)
    for k in range(16):
        u_send[k] = terms[:, 128 * k:128 * k + 128]
    u_slots[8 * core + y] = u_send[col]
    for d in (8, 9, 7, 6, 10, 5, 11, 4, 12, 3, 13, 2, 14, 1, 15):
        to = (col + d) % 16
        remote(
            u_send.at[to], u_slots.at[8 * core + y], stage_send.at[2], stage_recv.at[2],
            (row, to),
        ).start()
    arrived(s_full.at[pl.ds(0, 7)], stage_send.at[1])
    arrived(u_slots.at[pl.ds(0, 15)], stage_recv.at[2])
    for half in range(2):
        total = u_slots[8 * half]
        for d in range(1, NY):
            total = total + u_slots[8 * half + d]
        out[1, 8 * half:8 * half + 8, :] = total
    arrived(u_slots.at[pl.ds(0, 15)], stage_send.at[2])


def per_device(
    prior_solved, block_one, block_two, cross_block, inverse_one, inverse_two, rhs_one, rhs_two
):
    vmem = pltpu.VMEM
    dma = pltpu.SemaphoreType.DMA
    out = pl.pallas_call(
        kernel,
        out_shape=jax.ShapeDtypeStruct((2, 16, 128), F32),
        in_specs=[pl.BlockSpec(memory_space=pltpu.HBM)] * 8,
        out_specs=pl.BlockSpec(memory_space=pltpu.VMEM),
        scratch_shapes=[
            vmem((8, 2, 16, DEPTH), F32),
            vmem((2, 256, DEPTH), F32),
            vmem((2, 256, DEPTH), BF16),
            vmem((2, 256, DEPTH), BF16),
            vmem((2, 3, NX, NZ, 64, 128), F32),
            vmem((3, NX, 512, 256), BF16),
            vmem((3, NX, 512, 256), BF16),
            vmem((2, 2, 8, 128), F32),
            vmem((32, 8, 512), F32),
            vmem((NZ, NX, 8, 512), F32),
            vmem((NZ, 8, 512), F32),
            vmem((NZ, 8, 512), F32),
            vmem((NY, 8, 256), F32),
            vmem((NY - 1, 8, 256), F32),
            vmem((8, 256), F32),
            vmem((NY, 8, 256), F32),
            vmem((3, 8, 128), F32),
            vmem((16, 8, 128), F32),
            vmem((16, 8, 128), F32),
            dma((9,)),
            dma,
            dma((2, 14)),
            dma((9,)),
            dma((9,)),
            dma,
            dma((2,)),
            dma,
            dma,
            dma,
            dma((2, 4)),
            dma((2, 2, 2)),
            dma((2, 2, 2)),
            dma,
            dma((NZ,)),
            dma,
            dma,
            dma((3,)),
            dma((3,)),
        ],
        compiler_params=pltpu.CompilerParams(
            collective_id=0, has_side_effects=True, vmem_limit_bytes=62 * 1024 * 1024
        ),
    )(
        prior_solved.T, block_one, block_two, cross_block.T, inverse_one, inverse_two,
        rhs_one.T, rhs_two.T,
    )
    return out[0].T, out[1].T


def solution(mesh):
    placed = (
        P("row", "col"),
        P("col", "row"),
        P("col", "row"),
        P("col", "row"),
        P("row", "col"),
        P("row", "col"),
        P("col", "row"),
        P("col", "row"),
    )
    return jax.shard_map(
        per_device,
        mesh=mesh,
        in_specs=placed,
        out_specs=(P("col", "row"), P("col", "row")),
        check_vma=False,
    )
```

time: 73.5 us -> 70.9 us (0.965)
  Pallas kernels: 70.8 us -> 68.8 us
    pallas_call x1, Pallas kernels: 70.8 us -> 68.8 us  [per_device(): pl.pallas_call(kernel, out_shape=jax.ShapeDtypeStruct((2, 16, 128), F32),...]
    unnamed x4 -> x0, local copies, waits for them, and re-layouts: 1.9 us -> none
    transpose x0 -> x1, local copies, waits for them, and re-layouts: none -> 1.32 us  [per_device(): return (out[0].T, out[1].T)]
where the time goes in v3:
time: 70.9 us; the launch traced here: 70.8 us
  Pallas kernels  68.8 us (97%)
  local copies, waits for them, and re-layouts  1.32 us (2%)
    pallas_call x1, Pallas kernels, per_device(): pl.pallas_call(kernel, out_shape=jax.ShapeDtypeStruct((2, 16, 128), F32),...  68.8 us

profile of v3, /device:TPU:1, one launch (start us, length us, event | category | flops | bytes accessed | tf_op | source)
XLA Modules:
  0.0 70.8 jit_solution(1395929275345656208)
XLA Ops:
  0.6 68.8 %shard_map.95 = f32[2,16,128]{2,1,0:T(8,128)} custom-call(f32[32,1536]{1,0:T(8,128)} %bitcast.12, f32[128,1536]{1,0:T(8,128)} %block_one.1, f32[128,1536]{1,0:T(8,128)} %block_two.1, f32[64,128]{1,0:T(8,128)} %bitcast.13, f32[64,128]{1,0:T(8,128)} %inv_one.1, f32[64,128]{1,0:T(8,128)} %inv_two.1, f32[16,128]{1,0:T(8,128)} %bitcast.14, f32[16,128]{1,0:T(8,128)} %bitcast.15), custom_call_target="tpu_custom_call" | custom-call | tf_op jit(solution)/shard_map/pallas_call | solution.py:420
  69.4 1.3 %slice_bitcast_fusion = (f32[128,16]{0,1:T(8,128)}, f32[128,16]{0,1:T(8,128)}) fusion(f32[2,16,128]{2,1,0:T(8,128)} %shard_map.95), kind=kLoop, calls=%fused_computation | loop fusion | bytes 32768 | tf_op jit(solution)/shard_map/transpose | solution.py:472

commit v4 on v3

--- a/solution.py
+++ b/solution.py
@@ -8,9 +8,8 @@
 from jax.sharding import PartitionSpec as P
 
 NX, NZ, NY = 4, 8, 8
-C_AT = 0
-X_AT = (3, 5)
-RING_AT = (2, 5, 6)
+X_AT = 3
+RING_AT = ((0, 3, 5), (0, 4, 6))
 DEPTH = 1536
 MESH = pl.DeviceIdType.MESH
 F32 = jnp.float32
@@ -131,25 +130,27 @@
     def z_end(k):
         arrived(mats.at[core, k, x, pl.ds(0, 7)], zd_recv.at[k])
 
-    def two_start():
-        loads[2].wait()
-        ref = mats.at[core, 2, x, z]
+    def ring_start(k):
+        loads[k].wait()
+        ref = mats.at[core, k, x, z]
         for d in (2, 1, 3):
-            remote(ref, ref, xd_send, xd_recv, at((x + d) % NX, z, y, core)).start()
+            remote(
+                ref, ref, xd_send, xd_recv.at[k - 1], at((x + d) % NX, z, y, core)
+            ).start()
 
     z_next = (at(x, (z + 1) % NZ, y, core), at(x, (z + NZ - 1) % NZ, y, core))
 
-    def two_step(step):
+    def ring_step(k, step):
         if step == 0:
-            arrived(mats.at[core, 2, pl.ds(0, 3), z], xd_recv)
+            arrived(mats.at[core, k, pl.ds(0, 3), z], xd_recv.at[k - 1])
         for way in range(2):
             last = (4, 3)[way]
             owner = (z + NZ - step) % NZ if way == 0 else (z + step) % NZ
-            ref = mats.at[core, 2, pl.ds(0, NX), owner]
+            ref = mats.at[core, k, pl.ds(0, NX), owner]
             if 0 < step <= last:
-                arrived(ref, zr_recv.at[way, step - 1])
+                arrived(ref, zr_recv.at[k - 1, way, step - 1])
             if step < last:
-                remote(ref, ref, zr_send, zr_recv.at[way, step], z_next[way]).start()
+                remote(ref, ref, zr_send, zr_recv.at[k - 1, way, step], z_next[way]).start()
 
     x_next = (at((x + 1) % NX, z, y, core), at((x + 3) % NX, z, y, core))
     x_before = ((x + 3) % NX, (x + 1) % NX)
@@ -173,11 +174,6 @@
         remote(
             mats.at[core, k], mats.at[core, k], mate_send.at[4 + k], mate_recv.at[4 + k], mate
         ).start()
-
-    def x_end(k):
-        for way in range(2):
-            arrived(mats.at[core, k, (x + 2) % NX, pl.ds(4 * way, 4)], xr_recv.at[k, way, 1])
-        to_mate(k)
 
     def panel_rows(k, xx):
         both = jnp.concatenate(
@@ -209,7 +205,8 @@
         panel_rows(0, (x + 2) % NX)
 
     z_start(0)
-    two_start()
+    ring_start(1)
+    ring_start(2)
 
     def halves(c):
         for r in range(0, 256, 32):
@@ -295,13 +292,12 @@
                 product(0)
             if sub == 0 and i >= 2:
                 product(i - 1)
-        if i == C_AT:
-            z_start(1)
-        if i in RING_AT:
-            two_step(RING_AT.index(i))
-        if i in X_AT:
-            z_end(X_AT.index(i))
-            x_start(X_AT.index(i))
+        for k in range(1, 3):
+            if i in RING_AT[k - 1]:
+                ring_step(k, RING_AT[k - 1].index(i))
+        if i == X_AT:
+            z_end(0)
+            x_start(0)
     product(6)
     x_forward(0)
     for d in (0, 1, 3):
@@ -312,9 +308,9 @@
         over_z(4 * (1 - far) + t)
     for t in range(4):
         over_z(4 * far + t)
-    two_step(3)
+    ring_step(1, 3)
+    ring_step(2, 3)
     one_near()
-    x_forward(1)
     one_far()
 
     arrived(z_slots.at[pl.ds(1, NZ - 1)], q_recv)
@@ -343,9 +339,9 @@
             at(x, z, to, core),
         ).start()
 
-    x_end(1)
-    two_step(4)
-    to_mate(2)
+    for k in range(1, 3):
+        ring_step(k, 4)
+        to_mate(k)
     second = of_block(1)
     arrived(t_slots, stage_recv.at[0])
     total = t_send[y]
@@ -372,13 +368,12 @@
     arrived(slab.at[pl.ds(0, 7)], y_send)
     for hand in hands:
         hand.wait_send()
-    arrived(mats.at[core, pl.ds(0, 2), 0, pl.ds(0, 7)], zd_send)
-    arrived(mats.at[core, 2, pl.ds(0, 3), 0], xd_send)
-    arrived(mats.at[core, 2, pl.ds(0, 4), pl.ds(0, 7)], zr_send)
-    for k in range(2):
-        for way in range(2):
-            arrived(mats.at[core, k, x], xr_send.at[k, way, 0])
-            arrived(mats.at[core, k, x, pl.ds(0, 4)], xr_send.at[k, way, 1])
+    arrived(mats.at[core, 0, 0, pl.ds(0, 7)], zd_send)
+    arrived(mats.at[core, pl.ds(1, 2), pl.ds(0, 3), 0], xd_send)
+    arrived(mats.at[core, pl.ds(1, 2), pl.ds(0, 4), pl.ds(0, 7)], zr_send)
+    for way in range(2):
+        arrived(mats.at[core, 0, x], xr_send.at[0, way, 0])
+        arrived(mats.at[core, 0, x, pl.ds(0, 4)], xr_send.at[0, way, 1])
     arrived(mats.at[core, 0, pl.ds(0, 3)], mate_send.at[4])
     arrived(mats.at[core, 0, 0], mate_send.at[8])
     for k in range(1, 3):
@@ -448,13 +443,13 @@
             dma((9,)),
             dma((9,)),
             dma,
+            dma((1,)),
+            dma,
             dma((2,)),
             dma,
-            dma,
-            dma,
-            dma((2, 4)),
-            dma((2, 2, 2)),
-            dma((2, 2, 2)),
+            dma((2, 2, 4)),
+            dma((1, 2, 2)),
+            dma((1, 2, 2)),
             dma,
             dma((NZ,)),
             dma,

time: 70.9 us -> 66.7 us (0.941)
  Pallas kernels: 68.8 us -> 64.5 us
    pallas_call x1, Pallas kernels: 68.8 us -> 64.5 us  [per_device(): pl.pallas_call(kernel, out_shape=jax.ShapeDtypeStruct((2, 16, 128), F32),...]
where the time goes in v4:
time: 66.7 us; the launch traced here: 66.5 us
  Pallas kernels  64.5 us (97%)
  local copies, waits for them, and re-layouts  1.32 us (2%)
    pallas_call x1, Pallas kernels, per_device(): pl.pallas_call(kernel, out_shape=jax.ShapeDtypeStruct((2, 16, 128), F32),...  64.5 us

profile of v4, /device:TPU:1, one launch (start us, length us, event | category | flops | bytes accessed | tf_op | source)
XLA Modules:
  0.0 66.5 jit_solution(17803562116850803006)
XLA Ops:
  0.6 64.5 %shard_map.95 = f32[2,16,128]{2,1,0:T(8,128)} custom-call(f32[32,1536]{1,0:T(8,128)} %bitcast.12, f32[128,1536]{1,0:T(8,128)} %block_one.1, f32[128,1536]{1,0:T(8,128)} %block_two.1, f32[64,128]{1,0:T(8,128)} %bitcast.13, f32[64,128]{1,0:T(8,128)} %inv_one.1, f32[64,128]{1,0:T(8,128)} %inv_two.1, f32[16,128]{1,0:T(8,128)} %bitcast.14, f32[16,128]{1,0:T(8,128)} %bitcast.15), custom_call_target="tpu_custom_call" | custom-call | tf_op jit(solution)/shard_map/pallas_call | solution.py:415
  65.2 1.3 %slice_bitcast_fusion = (f32[128,16]{0,1:T(8,128)}, f32[128,16]{0,1:T(8,128)}) fusion(f32[2,16,128]{2,1,0:T(8,128)} %shard_map.95), kind=kLoop, calls=%fused_computation | loop fusion | bytes 32768 | tf_op jit(solution)/shard_map/transpose | solution.py:467
